TPU v7x, 256 devices: a whole 4x4x8 slice. The times are simulated.
256 devices in a mesh: seq: 64 (over x, y, z_hi, core), head: 4 (over z_lo).
Axes of the slice: x: 4, y: 4, z: 8 (z_hi: 2, z_lo: 4; z = z_hi * 4 + z_lo), core: 2. Of those that a mesh axis runs over, the one named last changes fastest.
Arguments:
- query_nope: bfloat16 [1, 64, 16384], P(None, 'seq', 'head'), may hold values from -6 to 6
- query_rope: bfloat16 [1, 64, 8192], P(None, 'seq', 'head'), may hold values from -8 to 8
- cache_latent: bfloat16 [1, 32768, 512], P(None, ('seq', 'head')), may hold values from -6 to 6
- cache_rope: bfloat16 [1, 32768, 64], P(None, ('seq', 'head')), may hold values from -8 to 8
- key_weight: bfloat16 [128, 128, 512], P('head'), may hold values from -0.5 to 0.5
- value_weight: bfloat16 [128, 512, 128], P('head'), may hold values from -0.25 to 0.25
- span_starts: int32 [1], replicated, may hold values from 32640 to 32704
Outputs:
- attended: bfloat16 [1, 64, 16384], P(None, 'seq', 'head')
Inputs may be any that keep to these rules, and one draw needn't show every extreme that they name: `span_starts`: each prompt's new tokens lie inside its cache.
All inputs are finite; a program needn't handle non-finite values.
Results may differ from a plain program's by a relative error of at most 0.0085.
The roundings to bfloat16 on the way count: a program that leaves them out, or rounds other values in their place, can miss the bound.
Values may be sent and summed in bfloat16 or wider, within the bound.
A program may use at most 64 MiB of HBM per device.

v0:
```python
import jax
import jax.numpy as jnp
from jax import lax
from jax.sharding import PartitionSpec as P

softmax_gain = 0.13524
floor_value = -1e30


def body(query_nope, query_rope, cache_latent, cache_rope, key_weight, value_weight, span_starts):
    head_count = key_weight.shape[0]
    nope_width = key_weight.shape[1]
    value_width = value_weight.shape[2]
    prompt_count = query_nope.shape[0]
    rope_width = cache_rope.shape[2]
    whole_nope, whole_rope = (
        lax.all_gather(query_nope, "seq", axis=1, tiled=True),
        lax.all_gather(query_rope, "seq", axis=1, tiled=True),
    )
    query_count = whole_nope.shape[1]
    split_nope = whole_nope.reshape(prompt_count, query_count, head_count, nope_width)
    absorbed = jnp.einsum(
        "bqhd,hdc->bqhc", split_nope, key_weight, preferred_element_type=jnp.float32
    ).astype(jnp.bfloat16)
    rotary = whole_rope.reshape(prompt_count, query_count, head_count, rope_width)
    group_rows = cache_latent.shape[1] * lax.axis_size("head")
    group_start = lax.axis_index("seq") * group_rows
    limit = span_starts[:, None] + jnp.arange(query_count, dtype=jnp.int32)[None, :]
    row_shape = (prompt_count, query_count, head_count)
    running_max = jnp.full(row_shape, floor_value, jnp.float32)
    latent_piece = lax.all_gather(cache_latent, "head", axis=1, tiled=True)
    rope_piece = lax.all_gather(cache_rope, "head", axis=1, tiled=True)
    scores = jnp.einsum(
        "bqhc,bpc->bqhp", absorbed, latent_piece, preferred_element_type=jnp.float32
    )
    scores = scores + jnp.einsum(
        "bqhr,bpr->bqhp", rotary, rope_piece, preferred_element_type=jnp.float32
    )
    position = group_start + jnp.arange(latent_piece.shape[1], dtype=jnp.int32)
    visible = position[None, None, None, :] <= limit[:, :, None, None]
    scores = jnp.where(visible, scores * softmax_gain, floor_value)
    new_max = jnp.maximum(running_max, jnp.max(scores, axis=-1))
    mass = jnp.where(visible, jnp.exp(scores - new_max[..., None]), 0.0)
    running_sum = jnp.sum(mass, axis=-1)
    update = jnp.einsum(
        "bqhp,bpc->bqhc",
        mass.astype(jnp.bfloat16),
        latent_piece,
        preferred_element_type=jnp.float32,
    )
    accumulated = update
    running_max, running_sum, accumulated = (new_max, running_sum, accumulated)
    overall_max = lax.pmax(running_max, "seq")
    factor = jnp.exp(running_max - overall_max)
    running_sum = running_sum * factor
    accumulated = accumulated * factor[..., None]
    summed, denom = (
        lax.psum_scatter(accumulated, "seq", scatter_dimension=1, tiled=True),
        lax.psum_scatter(running_sum, "seq", scatter_dimension=1, tiled=True),
    )
    mixed = summed / denom[..., None]
    output = jnp.einsum(
        "bqhc,hcv->bqhv", mixed, value_weight.astype(jnp.float32), precision=lax.Precision.HIGHEST
    )
    return output.reshape(prompt_count, output.shape[1], head_count * value_width).astype(
        jnp.bfloat16
    )


def solution(mesh):
    placed = (
        P(None, "seq", "head"),
        P(None, "seq", "head"),
        P(None, ("seq", "head"), None),
        P(None, ("seq", "head"), None),
        P("head", None, None),
        P("head", None, None),
        P(),
    )
    return jax.shard_map(
        body, mesh=mesh, in_specs=placed, out_specs=P(None, "seq", "head"), check_vma=False
    )
```

profile of v0, /device:TPU:1, one launch (start us, length us, event | category | flops | bytes accessed | tf_op | source)
XLA Modules:
  0.0 1107.0 jit_solution(9654517580067920488)
XLA Ops:
  6.5 0.0 copy-start.1
  6.5 0.0 reduce-scatter.3.cloned.1.call-start
  7.2 16.5 %all_gather.13 = bf16[1,512,512]{2,1,0:T(8,128)(2,1)S(1)} all-gather(bf16[1,128,512]{2,1,0:T(8,128)(2,1)} %param.9), channel_id=1, replica_groups=mesh['seq'=64,'head'=4] {'head'}, dimensions={1}, use_global_device_ids=true | all-gather | bytes 655360 | tf_op jit(solution)/shard_map/all_gather | solution.py:31
  23.7 124.3 %all_gather.12 = bf16[1,64,4096]{2,0,1:T(2,128)(2,1)S(1)} all-gather(bf16[1,1,4096]{2,0,1:T(2,128)(2,1)} %bitcast.54), channel_id=1, replica_groups=mesh['seq'=64,'head'=4] {'seq'}, dimensions={1}, use_global_device_ids=true | all-gather | bytes 532480 | tf_op jit(solution)/shard_map/all_gather | solution.py:17
  148.0 110.0 %all_gather.14 = bf16[1,64,2048]{2,0,1:T(2,128)(2,1)S(1)} all-gather(bf16[1,1,2048]{2,0,1:T(2,128)(2,1)} %bitcast.55), channel_id=1, replica_groups=mesh['seq'=64,'head'=4] {'seq'}, dimensions={1}, use_global_device_ids=true | all-gather | bytes 266240 | tf_op jit(solution)/shard_map/all_gather | solution.py:18
  258.0 3.1 reduce.4
  261.2 1.5 reduce.5
  262.7 0.5 reshape.128
  263.2 0.0 copy-done.1
  263.2 9.5 all_gather.15
  272.8 0.1 broadcast_compare_fusion
  272.9 2.9 convert_bitcast_fusion
  275.8 1.7 fusion.3
  277.5 2.9 fusion.18
  280.4 395.4 %pmax.7 = f32[1,64,32]{2,1,0:T(8,128)S(1)} all-reduce(f32[1,64,32]{2,1,0:T(8,128)S(1)} %get-tuple-element.8), channel_id=1, replica_groups=mesh['seq'=64,'head'=4] {'seq'}, use_global_device_ids=true, to_apply=%region_1.2 | all-reduce | flops 2048 | bytes 16384 | tf_op jit(solution)/shard_map/pmax | solution.py:53
  675.7 0.0 copy-start
  675.7 3.5 fusion
  679.3 0.0 copy-done
  679.3 2.9 multiply_bitcast_fusion
  682.1 0.0 copy-start.2
  682.1 0.0 reduce-scatter.3.cloned.1.call-update
  682.2 0.6 copy-done.2
  682.8 0.6 dynamic-slice
  683.4 401.0 %all-reduce = f32[1,64,32]{2,1,0:T(8,128)S(1)} all-reduce(f32[1,64,32]{2,1,0:T(8,128)S(1)} %get-tuple-element.5), channel_id=3, replica_groups=mesh['seq'=64,'head'=4] {'seq'}, use_global_device_ids=true, to_apply=%region_4.5.clone | all-reduce | flops 2048 | bytes 16384
  1084.4 0.7 dynamic-slice_bitcast_fusion
  1085.1 10.1 reduce-scatter.3.cloned.1.call-done
  1095.1 0.9 divide_bitcast_fusion
  1096.1 3.5 fusion.13
  1099.6 0.6 convert_element_type.33
  (5 shorter events, 0.0 us)
Async XLA Ops:
  6.5 256.7 %copy-start.1 = (bf16[1,128,64]{1,2,0:T(8,128)(2,1)S(1)}, bf16[1,128,64]{1,2,0:T(8,128)(2,1)}, u32[]{:S(2)}) copy-start(bf16[1,128,64]{1,2,0:T(8,128)(2,1)} %param.10) | copy-start | bytes 49156
  6.5 1088.6 %reduce-scatter.3.cloned.1.call-start = ((), (), s32[]{:S(2)}) async-start(), calls=%async_computation.1 | async-start | bytes 4259840 | tf_op jit(solution)/shard_map/reduce_scatter | solution.py:58
  675.7 3.5 copy-start
  682.1 0.7 copy-start.2
Sparse Core Ops, SparseCore 0:
  682.3 412.8 reduce-scatter.2
where the time goes:
time: 1120 us; the launch traced here: 1110 us
  blocking collectives  1060 us (95%)
  between operations  14.2 us (1%)
  matrix products  13.9 us (1%)
    unnamed x1, blocking collectives  401 us
    pmax x1, blocking collectives, body(): overall_max = lax.pmax(running_max, 'seq')  395 us
    all_gather x1, blocking collectives, body(): lax.all_gather(query_nope, 'seq', axis=1, tiled=True)  124 us
    all_gather x1, blocking collectives, body(): lax.all_gather(query_rope, 'seq', axis=1, tiled=True)  110 us
  transfers between devices with their start and end apart: 1, of which 1 were waited for; matrix products, arithmetic and copies ran while one was open for 0% of the time, Pallas kernels for 0%

commit v1 on v0

v1 whole, which is shorter than its diff:
```python
import jax
import jax.numpy as jnp
from jax import lax
from jax.experimental import pallas as pl
from jax.experimental.pallas import tpu as pltpu
from jax.sharding import PartitionSpec as P

MESH = pl.DeviceIdType.MESH
bf16, f32 = jnp.bfloat16, jnp.float32
gain = 0.13524
gain2 = gain * 1.4426950408889634
floor_value = -1e30

HEADS = 16
TOKENS = 32
ROWS = HEADS * TOKENS
BLOCK = 128
PARTS = 3


def coords():
    s, zl = lax.axis_index("seq"), lax.axis_index("head")
    return s // 16, (s // 4) % 4, ((s // 2) % 2) * 4 + zl, s % 2


def device(x, y, z, c):
    return (((x * 4 + y) * 2 + z // 4) * 2 + c, z % 4)


def remote(src, dst, send, recv, to):
    return pltpu.make_async_remote_copy(src, dst, send, recv, device_id=to, device_id_type=MESH)


def kernel(span_ref, qn_hbm, qr_hbm, lat_hbm, rope_hbm, kw_hbm, vw_hbm, out_ref,
           qn, qr, qtmp, qs, rq, qf, kw, vw, lat, rp, rx, rope_own, a_lat, a_rope, m_s, l_s, acc, of, mlf, so, ro,
           load_sem, q_send, q_recv, r_send, r_recv, c_send, c_recv, o_send, o_recv):
    x, y, z, c = coords()
    up, down = device(x, y, (z + 1) % 8, c), device(x, y, (z + 7) % 8, c)
    other = device(x, y, z, 1 - c)
    me = (x * 4 + y) * 2 + c
    peers = []
    for i in range(1, 32):
        dx, dy, dc = i // 8, (i // 2) % 4, i % 2
        px, py, pc = (x + dx) % 4, (y + dy) % 4, (c + dc) % 2
        peers.append((device(px, py, z, pc), (px * 4 + py) * 2 + pc, pc))

    barrier = pltpu.get_barrier_semaphore()
    for to in [p[0] for p in peers] + [up, down]:
        pl.semaphore_signal(barrier, inc=1, device_id=to, device_id_type=MESH)

    my_rows = pl.ds(pl.multiple_of(c * 128, 128), 128)
    loads = [
        pltpu.make_async_copy(qn_hbm, qn, load_sem.at[0]),
        pltpu.make_async_copy(qr_hbm, qr, load_sem.at[1]),
        pltpu.make_async_copy(rope_hbm.at[0], rope_own, load_sem.at[2]),
        pltpu.make_async_copy(lat_hbm.at[0], lat.at[z, my_rows], load_sem.at[3]),
        pltpu.make_async_copy(kw_hbm.at[pl.ds(c * HEADS, HEADS)], kw, load_sem.at[4]),
        pltpu.make_async_copy(vw_hbm.at[pl.ds(c * HEADS, HEADS)], vw, load_sem.at[5]),
    ]
    for copy in loads:
        copy.start()

    lane16 = lax.broadcasted_iota(jnp.int32, (16, 128), 1)
    loads[2].wait()
    eye = lax.broadcasted_iota(jnp.int32, (64, 128), 0) == lax.broadcasted_iota(jnp.int32, (64, 128), 1) % 64
    doubled = jnp.dot(rope_own[...], jnp.where(eye, 1.0, 0.0).astype(bf16), preferred_element_type=f32)
    rope_rows = pl.ds(pl.multiple_of(c * 16, 16), 16)
    for t in range(4):
        tile = jnp.where(lane16 < 64, doubled[32 * t : 32 * t + 16], doubled[32 * t + 16 : 32 * t + 32])
        rp[z, rope_rows, 128 * t : 128 * t + 128] = tile.astype(bf16)
    loads[0].wait()
    loads[1].wait()
    qtmp[...] = jnp.zeros_like(qtmp)
    nope_row, rope_row = qn[0].astype(f32), qr[0].astype(f32)
    for half in range(2):
        for h in range(HEADS):
            at = (half * HEADS + h) * 128
            qtmp[half, h : h + 1, :] = nope_row[:, at : at + 128]
        for h in range(HEADS // 2):
            at = (half * HEADS // 2 + h) * 128
            qtmp[half, 16 + h : 17 + h, :] = rope_row[:, at : at + 128]
    qs[...] = qtmp[...].astype(bf16)
    loads[3].wait()

    pl.semaphore_wait(barrier, 33)

    def part_of(slot, part):
        if part == 2:
            return rp.at[slot, rope_rows]
        return lat.at[slot, pl.ds(pl.multiple_of(c * 128 + 64 * part, 64), 64)]

    sent, ring, paired = [], {}, {}

    def ring_send(d, step, part):
        slot = (z + 8 - step) % 8 if d == 0 else (z + step) % 8
        ref = part_of(slot, part)
        copy = remote(ref, ref, r_send.at[d, step, part], r_recv.at[d, step, part], (up, down)[d])
        copy.start()
        ring[d, step, part] = copy
        sent.append(copy)

    def pair_send(d, step, part):
        slot = (z + 8 - step) % 8 if d == 0 else (z + step) % 8
        ref = part_of(slot, part)
        copy = remote(ref, ref, c_send.at[d, step, part], c_recv.at[d, step, part], other)
        copy.start()
        paired[d, step, part] = copy
        sent.append(copy)

    def ring_event(step, part):
        for d in range(2):
            if (d, step, part) in ring:
                ring[d, step, part].wait_recv()
                if step < 2 or (step == 2 and (d == 0) == (part != 1)):
                    ring_send(d, step + 1, part)
                pair_send(d, step + 1, part)

    for part in range(PARTS):
        for d in range(2):
            ring_send(d, 0, part)
        pair_send(0, 0, part)

    q_copies = []
    for i, (to, _, pc) in enumerate(peers):
        copy = remote(qs.at[pc], rq.at[me], q_send.at[i], q_recv.at[i], to)
        copy.start()
        q_copies.append(copy)
    rq[me] = qs[c]

    for part in range(PARTS):
        ring_event(0, part)

    loads[4].wait()
    for copy in q_copies:
        copy.wait_recv()

    lane_t = lax.broadcasted_iota(jnp.int32, (TOKENS, 128), 1)
    qf[...] = rq[...].reshape(TOKENS * 32, 128).astype(f32)
    for h in range(HEADS):
        rows = slice(h * TOKENS, (h + 1) * TOKENS)
        nope = qf[pl.ds(h, TOKENS, stride=32), :].astype(bf16)
        a_lat[rows, :] = jnp.dot(nope, kw[h], preferred_element_type=f32).astype(bf16)
        rope = qf[pl.ds(16 + h // 2, TOKENS, stride=32), :]
        a_rope[rows, :] = jnp.where((lane_t < 64) == (h % 2 == 0), rope, 0.0).astype(bf16)

    def unpack(slot):
        for cc in range(2):
            for t in range(4):
                tile = rp[slot, cc * 16 : cc * 16 + 16, 128 * t : 128 * t + 128].astype(f32)
                turned = pltpu.roll(tile, 64, 1)
                at = cc * 128 + 32 * t
                rx[slot, at : at + 16, :] = jnp.where(lane16 < 64, tile, turned).astype(bf16)
                rx[slot, at + 16 : at + 32, :] = jnp.where(lane16 < 64, turned, tile).astype(bf16)

    row = lax.broadcasted_iota(jnp.int32, (BLOCK, 128), 0) % TOKENS
    limit = span_ref[0] + (row // 2) * 4 + (z // 4) * 2 + row % 2
    column = lax.broadcasted_iota(jnp.int32, (BLOCK, 128), 1)

    def attend(block, slots, first):
        rows = pl.ds(block * BLOCK, BLOCK)
        tiles = []
        for slot in slots:
            s = lax.dot_general(a_lat[rows, :], lat[slot], (((1,), (1,)), ((), ())), preferred_element_type=f32)
            s += lax.dot_general(a_rope[rows, :], rx[slot], (((1,), (1,)), ((), ())), preferred_element_type=f32)
            for cc in range(2):
                base = ((((x * 4 + y) * 2 + slot // 4) * 2 + cc) * 4 + slot % 4) * 128
                tiles.append(jnp.where(column + base <= limit, s[:, cc * 128 : cc * 128 + 128], floor_value))
        top = tiles[0]
        for tile in tiles[1:]:
            top = jnp.maximum(top, tile)
        top = jnp.broadcast_to(jnp.max(top, axis=1, keepdims=True), (BLOCK, 128))
        if not first:
            before = m_s[rows, :]
            top = jnp.maximum(top, before)
            keep = jnp.exp2((before - top) * gain2)
        mass = [jnp.exp2((tile - top) * gain2) for tile in tiles]
        total = mass[0]
        for tile in mass[1:]:
            total = total + tile
        total = jnp.broadcast_to(jnp.sum(total, axis=1, keepdims=True), (BLOCK, 128))
        update = None
        for i, slot in enumerate(slots):
            weights = jnp.concatenate(mass[2 * i : 2 * i + 2], axis=1).astype(bf16)
            term = jnp.dot(weights, lat[slot], preferred_element_type=f32)
            update = term if update is None else update + term
        m_s[rows, :] = top
        if first:
            l_s[rows, :] = total
            acc[rows, :] = update
        else:
            l_s[rows, :] = l_s[rows, :] * keep + total
            for t in range(4):
                acc[rows, 128 * t : 128 * t + 128] = acc[rows, 128 * t : 128 * t + 128] * keep + update[:, 128 * t : 128 * t + 128]

    for step in range(5):
        if step in (0, 4):
            slots = [(z + step) % 8]
        else:
            slots = [(z + 8 - step) % 8, (z + step) % 8]
        for (d, s, part), copy in paired.items():
            if s == step:
                copy.wait_recv()
        for slot in slots:
            unpack(slot)
        for block in range(ROWS // BLOCK):
            attend(block, slots, step == 0)
            if block < PARTS and step < 3:
                ring_event(step + 1, block)

    loads[5].wait()
    lane = lax.broadcasted_iota(jnp.int32, (TOKENS, 128), 1)

    def split3(v):
        hi = v.astype(bf16).astype(f32)
        mid = (v - hi).astype(bf16).astype(f32)
        return hi, mid, v - hi - mid

    for h in range(HEADS):
        rows = slice(h * TOKENS, (h + 1) * TOKENS)
        of[pl.ds(h, TOKENS, stride=HEADS), :] = jnp.dot(acc[rows, :].astype(bf16), vw[h], preferred_element_type=f32)
        values = split3(m_s[rows, :]) + split3(l_s[rows, :])
        packed = jnp.zeros((TOKENS, 128), f32)
        for i, v in enumerate(values):
            packed = jnp.where(lane == i, v, packed)
        mlf[pl.ds(h, TOKENS, stride=HEADS), :] = packed
    so[:, 0:16, :] = of[...].reshape(TOKENS, HEADS, 128).astype(bf16)
    so[:, 16:32, :] = mlf[...].reshape(TOKENS, HEADS, 128).astype(bf16)
    o_copies = []
    for i, (to, token, _) in enumerate(peers):
        copy = remote(so.at[token], ro.at[me], o_send.at[i], o_recv.at[i], to)
        copy.start()
        o_copies.append(copy)
    ro[me] = so[me]
    for copy in o_copies:
        copy.wait_recv()

    for half in range(2):
        tops, sums = [], []
        for p in range(16):
            ml = ro[2 * p + half, 16:32, :].astype(f32)
            tops.append(jnp.sum(jnp.where(lane16 < 3, ml, 0.0), axis=1, keepdims=True))
            sums.append(jnp.sum(jnp.where((lane16 >= 3) & (lane16 < 6), ml, 0.0), axis=1, keepdims=True))
        top = tops[0]
        for t in tops[1:]:
            top = jnp.maximum(top, t)
        num, den = jnp.zeros((16, 128), f32), jnp.zeros((16, 1), f32)
        for p in range(16):
            scale = jnp.exp2((tops[p] - top) * gain2)
            num += scale * ro[2 * p + half, 0:16, :].astype(f32)
            den += scale * sums[p]
        out_ref[half * 16 : half * 16 + 16, :] = (num / den).astype(bf16)

    for copy in sent + q_copies + o_copies:
        copy.wait_send()


def body(query_nope, query_rope, cache_latent, cache_rope, key_weight, value_weight, span_starts):
    dma = pltpu.SemaphoreType.DMA
    vmem = pltpu.VMEM
    out = pl.pallas_call(
        kernel,
        out_shape=jax.ShapeDtypeStruct((32, 128), bf16),
        in_specs=[pl.BlockSpec(memory_space=pltpu.SMEM)] + [pl.BlockSpec(memory_space=pl.ANY)] * 6,
        out_specs=pl.BlockSpec(memory_space=pltpu.VMEM),
        scratch_shapes=[
            vmem((1, 1, 4096), bf16), vmem((1, 1, 2048), bf16), vmem((2, 32, 128), f32), vmem((2, 32, 128), bf16),
            vmem((32, 32, 128), bf16), vmem((1024, 128), f32), vmem((HEADS, 128, 512), bf16), vmem((HEADS, 512, 128), bf16),
            vmem((8, 256, 512), bf16), vmem((8, 32, 512), bf16), vmem((8, 256, 128), bf16), vmem((128, 64), bf16),
            vmem((ROWS, 512), bf16), vmem((ROWS, 128), bf16), vmem((ROWS, 128), f32), vmem((ROWS, 128), f32),
            vmem((ROWS, 512), f32), vmem((ROWS, 128), f32), vmem((ROWS, 128), f32),
            vmem((32, 32, 128), bf16), vmem((32, 32, 128), bf16),
            dma((6,)), dma((31,)), dma((31,)), dma((2, 4, PARTS)), dma((2, 4, PARTS)),
            dma((2, 5, PARTS)), dma((2, 5, PARTS)), dma((31,)), dma((31,)),
        ],
        compiler_params=pltpu.CompilerParams(collective_id=0, has_side_effects=True, vmem_limit_bytes=40 << 20),
        cost_estimate=pl.CostEstimate(flops=2 * 512 * 2048 * 1152, bytes_accessed=5 << 20, transcendentals=1 << 20),
    )(span_starts, query_nope, query_rope, cache_latent, cache_rope, key_weight, value_weight)
    return out.reshape(1, 1, 4096)


def solution(mesh):
    placed = (
        P(None, "seq", "head"),
        P(None, "seq", "head"),
        P(None, ("seq", "head"), None),
        P(None, ("seq", "head"), None),
        P("head", None, None),
        P("head", None, None),
        P(),
    )
    return jax.shard_map(
        body, mesh=mesh, in_specs=placed, out_specs=P(None, "seq", "head"), check_vma=False
    )
```

time: 1120 us -> 50.6 us (0.05); the launches traced: 1110 us -> 50.3 us
  blocking collectives: 1060 us -> 0 us
  Pallas kernels: 0 us -> 41.5 us
  matrix products: 13.9 us -> 0 us
  between operations: 14.2 us -> 0.68 us
    unnamed x1 -> x0, blocking collectives: 401 us -> none
    pmax x1 -> x0, blocking collectives: 395 us -> none  [body(): overall_max = lax.pmax(running_max, 'seq')]
    all_gather x4 -> x0, blocking collectives: 260 us -> none  [the longest x1 124 us: body(): lax.all_gather(query_nope, 'seq', axis=1, tiled=True)]
    pallas_call x0 -> x1, Pallas kernels: none -> 41.5 us  [body(): pl.pallas_call(kernel, out_shape=jax.ShapeDtypeStruct((32, 128), bf16), i...]
    dot_general x5 -> x0, matrix products: 13.9 us -> none  [the longest x1 3.5 us: body(): jnp.einsum('bqhc,hcv->bqhv', mixed, value_weight.astype(jnp.float32), pre...]
  transfers between devices with their start and end apart: 1 -> 0, of which waited for: 1 -> 0; matrix products, arithmetic and copies ran while one was open for 0% -> 0% of each run, Pallas kernels for 0% -> 0%
where the time goes in v1:
time: 50.6 us; the launch traced here: 50.3 us
  Pallas kernels  41.5 us (82%)
  local copies, waits for them, and re-layouts  8.14 us (16%)
  between operations  0.68 us (1%)
    pallas_call x1, Pallas kernels, body(): pl.pallas_call(kernel, out_shape=jax.ShapeDtypeStruct((32, 128), bf16), i...  41.5 us
    unnamed x11, local copies, waits for them, and re-layouts  7.52 us

profile of v1, /device:TPU:1, one launch (start us, length us, event | category | flops | bytes accessed | tf_op | source)
XLA Modules:
  0.0 50.3 jit_solution(14914817317113313571)
XLA Ops:
  0.7 0.8 %copy.8.rope_hbm = bf16[1,128,64]{2,1,0:T(8,128)(2,1)S(1)} copy(bf16[1,128,64]{1,2,0:T(8,128)(2,1)} %param.10) | data formatting | bytes 32768 | tf_op args[3]
  1.5 0.0 copy-start
  1.5 2.2 %copy-done = bf16[32,128,512]{2,1,0:T(8,128)(2,1)S(1)} copy-done((bf16[32,128,512]{2,1,0:T(8,128)(2,1)S(1)}, bf16[32,128,512]{2,1,0:T(8,128)(2,1)}, u32[]{:S(2)}) %copy-start) | copy-done | bytes 4194328
  3.7 0.0 copy-start.1
  3.7 2.2 %copy-done.1 = bf16[32,512,128]{2,1,0:T(8,128)(2,1)S(1)} copy-done((bf16[32,512,128]{2,1,0:T(8,128)(2,1)S(1)}, bf16[32,512,128]{2,1,0:T(8,128)(2,1)}, u32[]{:S(2)}) %copy-start.1) | copy-done | bytes 4194328
  5.9 0.0 copy-start.2
  5.9 0.9 %copy-done.2 = bf16[1,128,512]{2,1,0:T(8,128)(2,1)S(1)} copy-done((bf16[1,128,512]{2,1,0:T(8,128)(2,1)S(1)}, bf16[1,128,512]{2,1,0:T(8,128)(2,1)}, u32[]{:S(2)}) %copy-start.2) | copy-done | bytes 131096
  6.8 0.0 copy-start.3
  6.8 0.7 %copy-done.3 = bf16[1,1,4096]{2,1,0:T(2,128)(2,1)S(1)} copy-done((bf16[1,1,4096]{2,1,0:T(2,128)(2,1)S(1)}, bf16[1,1,4096]{2,1,0:T(2,128)(2,1)}, u32[]{:S(2)}) %copy-start.3) | copy-done | bytes 8216
  7.5 0.0 copy-start.4
  7.5 0.7 %copy-done.4 = bf16[1,1,2048]{2,1,0:T(2,128)(2,1)S(1)} copy-done((bf16[1,1,2048]{2,1,0:T(2,128)(2,1)S(1)}, bf16[1,1,2048]{2,1,0:T(2,128)(2,1)}, u32[]{:S(2)}) %copy-start.4) | copy-done | bytes 4120
  8.2 41.5 %shard_map.73 = bf16[32,128]{1,0:T(8,128)(2,1)S(1)} custom-call(s32[1]{0:T(128)S(6)} %copy.9.span_ref, bf16[1,1,4096]{2,1,0:T(2,128)(2,1)S(1)} %copy-done.3, bf16[1,1,2048]{2,1,0:T(2,128)(2,1)S(1)} %copy-done.4, bf16[1,128,512]{2,1,0:T(8,128)(2,1)S(1)} %copy-done.2, bf16[1,128,64]{2,1,0:T(8,128)(2,1)S(1)} %copy.8.rope_hbm, ...), custom_call_target="tpu_custom_call" | custom-call | flops 2415919104 | bytes 5242880 | tf_op jit(solution)/shard_map/pallas_call | solution.py:260
  49.7 0.6 %reshape.3 = bf16[1,1,4096]{2,1,0:T(2,128)(2,1)} reshape(bf16[32,128]{1,0:T(8,128)(2,1)S(1)} %shard_map.73) | data formatting | bytes 16384 | tf_op jit(solution)/shard_map/reshape | solution.py:278
Async XLA Ops:
  1.5 2.2 %copy-start = (bf16[32,128,512]{2,1,0:T(8,128)(2,1)S(1)}, bf16[32,128,512]{2,1,0:T(8,128)(2,1)}, u32[]{:S(2)}) copy-start(bf16[32,128,512]{2,1,0:T(8,128)(2,1)} %kw_hbm.1) | copy-start | bytes 12582916
  3.7 2.2 %copy-start.1 = (bf16[32,512,128]{2,1,0:T(8,128)(2,1)S(1)}, bf16[32,512,128]{2,1,0:T(8,128)(2,1)}, u32[]{:S(2)}) copy-start(bf16[32,512,128]{2,1,0:T(8,128)(2,1)} %vw_hbm.1) | copy-start | bytes 12582916
  5.9 0.9 %copy-start.2 = (bf16[1,128,512]{2,1,0:T(8,128)(2,1)S(1)}, bf16[1,128,512]{2,1,0:T(8,128)(2,1)}, u32[]{:S(2)}) copy-start(bf16[1,128,512]{2,1,0:T(8,128)(2,1)} %lat_hbm.1) | copy-start | bytes 393220
  6.8 0.7 %copy-start.3 = (bf16[1,1,4096]{2,1,0:T(2,128)(2,1)S(1)}, bf16[1,1,4096]{2,1,0:T(2,128)(2,1)}, u32[]{:S(2)}) copy-start(bf16[1,1,4096]{2,1,0:T(2,128)(2,1)} %qn_hbm.1) | copy-start | bytes 24580
  7.5 0.7 %copy-start.4 = (bf16[1,1,2048]{2,1,0:T(2,128)(2,1)S(1)}, bf16[1,1,2048]{2,1,0:T(2,128)(2,1)}, u32[]{:S(2)}) copy-start(bf16[1,1,2048]{2,1,0:T(2,128)(2,1)} %qr_hbm.1) | copy-start | bytes 12292

commit v2 on v0

v2 whole, which is shorter than its diff:
```python
import jax
import jax.numpy as jnp
from jax import lax
from jax.experimental import pallas as pl
from jax.experimental.pallas import tpu as pltpu
from jax.sharding import PartitionSpec as P

MESH = pl.DeviceIdType.MESH
bf16, f32 = jnp.bfloat16, jnp.float32
gain = 0.13524
gain2 = gain * 1.4426950408889634
floor_value = -1e30

HEADS = 16
TOKENS = 32
SIDE = HEADS * TOKENS
BLOCK = 128
PARTS = 3
ORDER = sorted(
    ((dx, dy) for dx in range(4) for dy in range(4) if dx or dy), key=lambda d: -min(d[0], 4 - d[0]) - min(d[1], 4 - d[1])
)


def coords():
    s, zl = lax.axis_index("seq"), lax.axis_index("head")
    return s // 16, (s // 4) % 4, ((s // 2) % 2) * 4 + zl, s % 2


def device(x, y, z, c):
    return (((x * 4 + y) * 2 + z // 4) * 2 + c, z % 4)


def remote(src, dst, send, recv, to):
    return pltpu.make_async_remote_copy(src, dst, send, recv, device_id=to, device_id_type=MESH)


def split3(v):
    hi = v.astype(bf16).astype(f32)
    mid = (v - hi).astype(bf16).astype(f32)
    return hi, mid, v - hi - mid


def pack_stats(stats):
    lane = lax.broadcasted_iota(jnp.int32, (16, 128), 1)
    packed = jnp.zeros((16, 128), f32)
    for i, v in enumerate(part for stat in stats for part in split3(stat)):
        packed = jnp.where(lane == i, v, packed)
    return packed


def merge(parts):
    lane = lax.broadcasted_iota(jnp.int32, (16, 128), 1)
    tops, totals = [], []
    for _, stats, at in parts:
        stats = stats.astype(f32)
        tops.append(jnp.sum(jnp.where((lane >= at) & (lane < at + 3), stats, 0.0), axis=1, keepdims=True))
        totals.append(jnp.sum(jnp.where((lane >= at + 3) & (lane < at + 6), stats, 0.0), axis=1, keepdims=True))
    top = tops[0]
    for t in tops[1:]:
        top = jnp.maximum(top, t)
    num, den = jnp.zeros((16, 128), f32), jnp.zeros((16, 1), f32)
    for (sums, _, _), t, total in zip(parts, tops, totals):
        scale = jnp.exp2((t - top) * gain2)
        num += scale * sums.astype(f32)
        den += scale * total
    return num, top, den


def kernel(span_ref, qn_hbm, qr_hbm, lat_hbm, rope_hbm, kw_hbm, vw_hbm, out_ref,
           qn, qr, qtmp, qs, qc, qm, rq, qf, kw, vw, lat, rp, rx, a_lat, a_rope, m_s, l_s, acc, of, so, ro, mm, fin,
           load_sem, q_send, q_recv, z_send, z_recv, f_send, f_recv, r_send, r_recv, c_send, c_recv, o_send, o_recv):
    x, y, z, c = coords()
    up, down = device(x, y, (z + 1) % 8, c), device(x, y, (z + 7) % 8, c)
    onward = device(x, y, (z + 1 + 6 * c) % 8, c)
    far = [device(x, y, (z + 4) % 8, c), device(x, y, (z + 4) % 8, 1 - c)]
    other = device(x, y, z, 1 - c)
    me = x * 4 + y
    peers = []
    for dx, dy in ORDER:
        px, py = (x + dx) % 4, (y + dy) % 4
        peers.append((device(px, py, z, c), px * 4 + py))

    rows_of = pl.ds(pl.multiple_of(c * 128, 128), 128)
    loads = [
        pltpu.make_async_copy(qn_hbm, qn, load_sem.at[0]),
        pltpu.make_async_copy(qr_hbm, qr, load_sem.at[1]),
        pltpu.make_async_copy(rope_hbm.at[0], rp.at[0, c], load_sem.at[2]),
        pltpu.make_async_copy(lat_hbm.at[0], lat.at[0, rows_of], load_sem.at[3]),
        pltpu.make_async_copy(kw_hbm.at[pl.ds(c * HEADS, HEADS)], kw, load_sem.at[4]),
        pltpu.make_async_copy(vw_hbm.at[pl.ds(c * HEADS, HEADS)], vw, load_sem.at[5]),
    ]
    for copy in loads:
        copy.start()

    barrier = pltpu.get_barrier_semaphore()
    for to in far + [up, down, other] + [p[0] for p in peers]:
        pl.semaphore_signal(barrier, inc=1, device_id=to, device_id_type=MESH)

    loads[0].wait()
    loads[1].wait()
    qtmp[...] = jnp.zeros_like(qtmp)
    nope_row, rope_row = qn[0].astype(f32), qr[0].astype(f32)
    for half in range(2):
        for h in range(HEADS):
            at = (half * HEADS + h) * 128
            qtmp[half, h : h + 1, :] = nope_row[:, at : at + 128]
        for h in range(HEADS // 2):
            at = (half * HEADS // 2 + h) * 128
            qtmp[half, pl.ds(16 + 8 * c + h, 1), :] = rope_row[:, at : at + 128]
    qs[...] = qtmp[...].astype(bf16)
    loads[2].wait()
    loads[3].wait()

    pl.semaphore_wait(barrier, 20)

    started = []

    def start(copy):
        copy.start()
        started.append(copy)
        return copy

    def piece(slot, part):
        if part == 2:
            return rp.at[slot, c]
        return lat.at[slot, pl.ds(pl.multiple_of(c * 128 + 64 * part, 64), 64)]

    def pair(slot, part):
        ref = piece(slot, part)
        return start(remote(ref, ref, c_send.at[slot, part], c_recv.at[slot, part], other))

    to_far = [
        start(remote(qs.at[c], qc.at[1, c], z_send.at[0], z_recv.at[0], far[0])),
        start(remote(qs.at[1 - c], qc.at[1, c], z_send.at[1], z_recv.at[1], far[1])),
    ]
    to_other = start(remote(qs.at[1 - c], qc.at[0, c], z_send.at[2], z_recv.at[2], other))
    qc[0, c] = qs[c]
    hop1, hop2, paired = {}, {}, []
    for part in range(PARTS):
        for d, to in enumerate((up, down)):
            hop1[d, part] = start(
                remote(piece(0, part), piece(1 + d, part), r_send.at[d, part], r_recv.at[d, part], to)
            )

    def send_queries(side):
        for core in range(2):
            qm[side, core] = qc[side, core, 0:16, :]
        qm[side, 2] = qc[side, 0, 16:32, :] + qc[side, 1, 16:32, :]
        copies = []
        for i, (to, _) in enumerate(peers):
            copies.append(start(remote(qm.at[side], rq.at[side, me], q_send.at[side, i], q_recv.at[side, i], to)))
        rq[side, me] = qm[side]
        return copies

    for part in range(PARTS):
        paired.append(pair(0, part))
    to_other.wait_recv()
    own_queries = send_queries(0)

    def arrive(part):
        for d in range(2):
            hop1[d, part].wait_recv()
        hop2[part] = start(
            remote(piece(1 + c, part), piece(3, part), r_send.at[2, part], r_recv.at[2, part], onward)
        )
        for d in range(2):
            paired.append(pair(1 + d, part))

    for copy in to_far:
        copy.wait_recv()
    far_queries = send_queries(1)
    for part in range(PARTS):
        arrive(part)

    lane_t = lax.broadcasted_iota(jnp.int32, (TOKENS, 128), 1)

    def by_head(row):
        return [qf[pl.ds(row[core], 16, stride=48), :] for core in range(2)]

    def absorb(side):
        qf[...] = rq[side].reshape(16 * 48, 128).astype(f32)
        for h in range(HEADS):
            rows = slice(side * SIDE + h * TOKENS, side * SIDE + (h + 1) * TOKENS)
            nope = jnp.concatenate(by_head((h, 16 + h)), axis=0).astype(bf16)
            a_lat[rows, :] = jnp.dot(nope, kw[h], preferred_element_type=f32).astype(bf16)
            rope = jnp.concatenate(by_head((32 + h // 2, 40 + h // 2)), axis=0)
            a_rope[rows, :] = jnp.where((lane_t < 64) == (h % 2 == 0), rope, 0.0).astype(bf16)

    def double_keys(slot):
        for cc in range(2):
            for twice in range(2):
                at = 256 * slot + 128 * cc
                rx[64 * twice : 64 * twice + 64, at : at + 128] = rp[slot, cc]

    row = lax.broadcasted_iota(jnp.int32, (BLOCK, 128), 0) % TOKENS
    column = lax.broadcasted_iota(jnp.int32, (BLOCK, 128), 1)

    def attend(side, block, low, high, first):
        rows = pl.ds(side * SIDE + block * BLOCK, BLOCK)
        z_hi = (z // 4 + side) % 2
        limit = span_ref[0] + (row % 16) * 4 + z_hi * 2 + row // 16 - column
        keys = lat[low:high].reshape((high - low) * 256, 512)
        s = lax.dot_general(a_lat[rows, :], keys, (((1,), (1,)), ((), ())), preferred_element_type=f32)
        s += jnp.dot(a_rope[rows, :], rx[:, 256 * low : 256 * high], preferred_element_type=f32)
        tiles = []
        for slot in range(low, high):
            for cc in range(2):
                zz = (z + (0, 7, 1, (6, 2)[cc])[slot]) % 8
                base = ((((x * 4 + y) * 2 + zz // 4) * 2 + cc) * 4 + zz % 4) * 128
                at = 128 * len(tiles)
                tiles.append(jnp.where(limit >= base, s[:, at : at + 128], floor_value))
        top = tiles[0]
        for tile in tiles[1:]:
            top = jnp.maximum(top, tile)
        top = jnp.broadcast_to(jnp.max(top, axis=1, keepdims=True), (BLOCK, 128))
        if not first:
            before = m_s[rows, :]
            top = jnp.maximum(top, before)
            keep = jnp.exp2((before - top) * gain2)
        mass = [jnp.exp2((tile - top) * gain2) for tile in tiles]
        total = mass[0]
        for tile in mass[1:]:
            total = total + tile
        total = jnp.broadcast_to(jnp.sum(total, axis=1, keepdims=True), (BLOCK, 128))
        update = jnp.dot(jnp.concatenate(mass, axis=1).astype(bf16), keys, preferred_element_type=f32)
        m_s[rows, :] = top
        if first:
            l_s[rows, :] = total
            acc[rows, :] = update
        else:
            l_s[rows, :] = l_s[rows, :] * keep + total
            for t in range(4):
                at = slice(128 * t, 128 * t + 128)
                acc[rows, at] = acc[rows, at] * keep + update[:, at]

    def send_partials(side):
        for h in range(HEADS):
            rows = slice(side * SIDE + h * TOKENS, side * SIDE + (h + 1) * TOKENS)
            result = jnp.dot(acc[rows, :].astype(bf16), vw[h], preferred_element_type=f32)
            stats = []
            for core in range(2):
                of[pl.ds(16 * core + h, 16, stride=48), :] = result[16 * core : 16 * core + 16]
                at = slice(rows.start + 16 * core, rows.start + 16 * core + 16)
                stats += [m_s[at, :], l_s[at, :]]
            of[pl.ds(32 + h, 16, stride=48), :] = pack_stats(stats)
        so[side] = of[...].reshape(16, 48, 128).astype(bf16)
        copies = []
        for i, (to, p) in enumerate(peers):
            copies.append(
                start(remote(so.at[side, p], ro.at[side, me], o_send.at[side, i], o_recv.at[side, i], to))
            )
        ro[side, me] = so[side, me]
        return copies

    loads[4].wait()
    for copy in own_queries:
        copy.wait_recv()
    absorb(0)
    for copy in paired:
        copy.wait_recv()
    for slot in range(3):
        double_keys(slot)
    for block in range(SIDE // BLOCK):
        attend(0, block, 0, 3, True)

    last = []
    for part in range(PARTS):
        hop2[part].wait_recv()
        last.append(pair(3, part))
    for copy in far_queries:
        copy.wait_recv()
    absorb(1)
    for block in range(SIDE // BLOCK):
        attend(1, block, 0, 3, True)
    for copy in last:
        copy.wait_recv()
    double_keys(3)
    for block in range(SIDE // BLOCK):
        attend(1, block, 3, 4, False)
    loads[5].wait()
    far_partials = send_partials(1)
    for block in range(SIDE // BLOCK):
        attend(0, block, 3, 4, False)
    own_partials = send_partials(0)

    def merge_plane(side):
        for core in range(2):
            num, top, den = merge(
                [(ro[side, p, 16 * core : 16 * core + 16, :], ro[side, p, 32:48, :], 6 * core) for p in range(16)]
            )
            mm[side, core, 0:16, :] = num.astype(bf16)
            mm[side, core, 16:32, :] = pack_stats([top, den]).astype(bf16)

    for copy in far_partials:
        copy.wait_recv()
    merge_plane(1)
    finals = [
        start(remote(mm.at[1, c], fin.at[1, c], f_send.at[0], f_recv.at[0], far[0])),
        start(remote(mm.at[1, 1 - c], fin.at[1, c], f_send.at[1], f_recv.at[1], far[1])),
    ]
    for copy in own_partials:
        copy.wait_recv()
    merge_plane(0)
    finals.append(start(remote(mm.at[0, 1 - c], fin.at[0, c], f_send.at[2], f_recv.at[2], other)))
    fin[0, c] = mm[0, c]
    for copy in finals:
        copy.wait_recv()
    for half in range(2):
        num, _, den = merge([(fin[source, half, 0:16, :], fin[source, half, 16:32, :], 0) for source in range(2)])
        out_ref[half * 16 : half * 16 + 16, :] = (num / den).astype(bf16)

    for copy in started:
        copy.wait_send()


def body(query_nope, query_rope, cache_latent, cache_rope, key_weight, value_weight, span_starts):
    dma = pltpu.SemaphoreType.DMA
    vmem = pltpu.VMEM
    out = pl.pallas_call(
        kernel,
        out_shape=pltpu.VMEM((32, 128), bf16),
        in_specs=[pl.BlockSpec(memory_space=pltpu.SMEM)] + [pl.BlockSpec(memory_space=pl.ANY)] * 6,
        out_specs=pl.BlockSpec(memory_space=pltpu.VMEM),
        scratch_shapes=[
            vmem((1, 1, 4096), bf16), vmem((1, 1, 2048), bf16), vmem((2, 32, 128), f32), vmem((2, 32, 128), bf16),
            vmem((2, 2, 32, 128), bf16), vmem((2, 3, 16, 128), bf16), vmem((2, 16, 3, 16, 128), bf16), vmem((768, 128), f32),
            vmem((HEADS, 128, 512), bf16), vmem((HEADS, 512, 128), bf16),
            vmem((4, 256, 512), bf16), vmem((4, 2, 64, 128), bf16), vmem((128, 1024), bf16),
            vmem((2 * SIDE, 512), bf16), vmem((2 * SIDE, 128), bf16), vmem((2 * SIDE, 128), f32), vmem((2 * SIDE, 128), f32),
            vmem((2 * SIDE, 512), f32), vmem((768, 128), f32),
            vmem((2, 16, 48, 128), bf16), vmem((2, 16, 48, 128), bf16), vmem((2, 2, 32, 128), bf16), vmem((2, 2, 32, 128), bf16),
            dma((6,)), dma((2, 15)), dma((2, 15)), dma((3,)), dma((3,)), dma((3,)), dma((3,)), dma((3, PARTS)), dma((3, PARTS)),
            dma((4, PARTS)), dma((4, PARTS)), dma((2, 15)), dma((2, 15)),
        ],
        compiler_params=pltpu.CompilerParams(collective_id=0, has_side_effects=True, vmem_limit_bytes=63 << 20),
        cost_estimate=pl.CostEstimate(flops=2 * 1024 * 1024 * 1152, bytes_accessed=5 << 20, transcendentals=1 << 20),
    )(span_starts, query_nope, query_rope, cache_latent, jnp.swapaxes(cache_rope, 1, 2), key_weight, value_weight)
    return out.reshape(1, 1, 4096)


def solution(mesh):
    placed = (
        P(None, "seq", "head"),
        P(None, "seq", "head"),
        P(None, ("seq", "head"), None),
        P(None, ("seq", "head"), None),
        P("head", None, None),
        P("head", None, None),
        P(),
    )
    return jax.shard_map(
        body, mesh=mesh, in_specs=placed, out_specs=P(None, "seq", "head"), check_vma=False
    )
```

time: 1120 us -> 40.2 us (0.04); the launches traced: 1110 us -> 40 us
  blocking collectives: 1060 us -> 0 us
  Pallas kernels: 0 us -> 38.7 us
  matrix products: 13.9 us -> 0 us
  between operations: 14.2 us -> 0.66 us
    unnamed x1 -> x0, blocking collectives: 401 us -> none
    pmax x1 -> x0, blocking collectives: 395 us -> none  [body(): overall_max = lax.pmax(running_max, 'seq')]
    all_gather x4 -> x0, blocking collectives: 260 us -> none  [the longest x1 124 us: body(): lax.all_gather(query_nope, 'seq', axis=1, tiled=True)]
    pallas_call x0 -> x1, Pallas kernels: none -> 38.7 us  [body(): pl.pallas_call(kernel, out_shape=pltpu.VMEM((32, 128), bf16), in_specs=[p...]
    dot_general x5 -> x0, matrix products: 13.9 us -> none  [the longest x1 3.5 us: body(): jnp.einsum('bqhc,hcv->bqhv', mixed, value_weight.astype(jnp.float32), pre...]
  transfers between devices with their start and end apart: 1 -> 0, of which waited for: 1 -> 0; matrix products, arithmetic and copies ran while one was open for 0% -> 0% of each run, Pallas kernels for 0% -> 0%
where the time goes in v2:
time: 40.2 us; the launch traced here: 40 us
  Pallas kernels  38.7 us (96%)
  between operations  0.66 us (2%)
  local copies, waits for them, and re-layouts  0.62 us (2%)
    pallas_call x1, Pallas kernels, body(): pl.pallas_call(kernel, out_shape=pltpu.VMEM((32, 128), bf16), in_specs=[p...  38.7 us

profile of v2, /device:TPU:1, one launch (start us, length us, event | category | flops | bytes accessed | tf_op | source)
XLA Modules:
  0.0 40.0 jit_solution(10744452689850091034)
XLA Ops:
  0.7 38.7 %shard_map.73 = bf16[32,128]{1,0:T(8,128)(2,1)S(1)} custom-call(s32[1]{0:T(128)S(6)} %copy.8.span_ref, bf16[1,1,4096]{2,1,0:T(2,128)(2,1)} %qn_hbm.1, bf16[1,1,2048]{2,1,0:T(2,128)(2,1)} %qr_hbm.1, bf16[1,128,512]{2,1,0:T(8,128)(2,1)} %lat_hbm.1, bf16[1,64,128]{2,1,0:T(8,128)(2,1)} %bitcast.1, bf16[32,128,512]{2,1,0:T(8,128)(2,1)} %kw_hbm.1, ...), custom_call_target="tpu_custom_call" | custom-call | flops 2415919104 | bytes 5242880 | tf_op jit(solution)/shard_map/pallas_call | solution.py:319
  39.4 0.6 %reshape.3 = bf16[1,1,4096]{2,1,0:T(2,128)(2,1)} reshape(bf16[32,128]{1,0:T(8,128)(2,1)S(1)} %shard_map.73) | data formatting | bytes 16384 | tf_op jit(solution)/shard_map/reshape | solution.py:338

commit v3 on v2

--- a/solution.py
+++ b/solution.py
@@ -14,7 +14,7 @@
 HEADS = 16
 TOKENS = 32
 SIDE = HEADS * TOKENS
-BLOCK = 128
+BLOCK = 512
 PARTS = 3
 ORDER = sorted(
     ((dx, dy) for dx in range(4) for dy in range(4) if dx or dy), key=lambda d: -min(d[0], 4 - d[0]) - min(d[1], 4 - d[1])
@@ -71,7 +71,6 @@
            load_sem, q_send, q_recv, z_send, z_recv, f_send, f_recv, r_send, r_recv, c_send, c_recv, o_send, o_recv):
     x, y, z, c = coords()
     up, down = device(x, y, (z + 1) % 8, c), device(x, y, (z + 7) % 8, c)
-    onward = device(x, y, (z + 1 + 6 * c) % 8, c)
     far = [device(x, y, (z + 4) % 8, c), device(x, y, (z + 4) % 8, 1 - c)]
     other = device(x, y, z, 1 - c)
     me = x * 4 + y
@@ -79,6 +78,10 @@
     for dx, dy in ORDER:
         px, py = (x + dx) % 4, (y + dy) % 4
         peers.append((device(px, py, z, c), px * 4 + py))
+
+    barrier = pltpu.get_barrier_semaphore()
+    for to in far + [up, down, other] + [p[0] for p in peers]:
+        pl.semaphore_signal(barrier, inc=1, device_id=to, device_id_type=MESH)
 
     rows_of = pl.ds(pl.multiple_of(c * 128, 128), 128)
     loads = [
@@ -91,10 +94,6 @@
     ]
     for copy in loads:
         copy.start()
-
-    barrier = pltpu.get_barrier_semaphore()
-    for to in far + [up, down, other] + [p[0] for p in peers]:
-        pl.semaphore_signal(barrier, inc=1, device_id=to, device_id_type=MESH)
 
     loads[0].wait()
     loads[1].wait()
@@ -160,9 +159,9 @@
     def arrive(part):
         for d in range(2):
             hop1[d, part].wait_recv()
-        hop2[part] = start(
-            remote(piece(1 + c, part), piece(3, part), r_send.at[2, part], r_recv.at[2, part], onward)
-        )
+            hop2[d, part] = start(
+                remote(piece(1 + d, part), piece(3 + d, part), r_send.at[2 + d, part], r_recv.at[2 + d, part], (up, down)[d])
+            )
         for d in range(2):
             paired.append(pair(1 + d, part))
 
@@ -205,7 +204,7 @@
         tiles = []
         for slot in range(low, high):
             for cc in range(2):
-                zz = (z + (0, 7, 1, (6, 2)[cc])[slot]) % 8
+                zz = (z + (0, 7, 1, 6, 2)[slot]) % 8
                 base = ((((x * 4 + y) * 2 + zz // 4) * 2 + cc) * 4 + zz % 4) * 128
                 at = 128 * len(tiles)
                 tiles.append(jnp.where(limit >= base, s[:, at : at + 128], floor_value))
@@ -263,24 +262,24 @@
     for block in range(SIDE // BLOCK):
         attend(0, block, 0, 3, True)
 
-    last = []
-    for part in range(PARTS):
-        hop2[part].wait_recv()
-        last.append(pair(3, part))
     for copy in far_queries:
         copy.wait_recv()
     absorb(1)
     for block in range(SIDE // BLOCK):
         attend(1, block, 0, 3, True)
-    for copy in last:
-        copy.wait_recv()
-    double_keys(3)
-    for block in range(SIDE // BLOCK):
-        attend(1, block, 3, 4, False)
     loads[5].wait()
     far_partials = send_partials(1)
+    last = []
+    for part in range(PARTS):
+        for d in range(2):
+            hop2[d, part].wait_recv()
+            last.append(pair(3 + d, part))
+    for copy in last:
+        copy.wait_recv()
+    for slot in (3, 4):
+        double_keys(slot)
     for block in range(SIDE // BLOCK):
-        attend(0, block, 3, 4, False)
+        attend(0, block, 3, 5, False)
     own_partials = send_partials(0)
 
     def merge_plane(side):
@@ -325,12 +324,12 @@
             vmem((1, 1, 4096), bf16), vmem((1, 1, 2048), bf16), vmem((2, 32, 128), f32), vmem((2, 32, 128), bf16),
             vmem((2, 2, 32, 128), bf16), vmem((2, 3, 16, 128), bf16), vmem((2, 16, 3, 16, 128), bf16), vmem((768, 128), f32),
             vmem((HEADS, 128, 512), bf16), vmem((HEADS, 512, 128), bf16),
-            vmem((4, 256, 512), bf16), vmem((4, 2, 64, 128), bf16), vmem((128, 1024), bf16),
+            vmem((5, 256, 512), bf16), vmem((5, 2, 64, 128), bf16), vmem((128, 1280), bf16),
             vmem((2 * SIDE, 512), bf16), vmem((2 * SIDE, 128), bf16), vmem((2 * SIDE, 128), f32), vmem((2 * SIDE, 128), f32),
             vmem((2 * SIDE, 512), f32), vmem((768, 128), f32),
             vmem((2, 16, 48, 128), bf16), vmem((2, 16, 48, 128), bf16), vmem((2, 2, 32, 128), bf16), vmem((2, 2, 32, 128), bf16),
-            dma((6,)), dma((2, 15)), dma((2, 15)), dma((3,)), dma((3,)), dma((3,)), dma((3,)), dma((3, PARTS)), dma((3, PARTS)),
-            dma((4, PARTS)), dma((4, PARTS)), dma((2, 15)), dma((2, 15)),
+            dma((6,)), dma((2, 15)), dma((2, 15)), dma((3,)), dma((3,)), dma((3,)), dma((3,)), dma((4, PARTS)), dma((4, PARTS)),
+            dma((5, PARTS)), dma((5, PARTS)), dma((2, 15)), dma((2, 15)),
         ],
         compiler_params=pltpu.CompilerParams(collective_id=0, has_side_effects=True, vmem_limit_bytes=63 << 20),
         cost_estimate=pl.CostEstimate(flops=2 * 1024 * 1024 * 1152, bytes_accessed=5 << 20, transcendentals=1 << 20),

time: 40.2 us -> 36.5 us (0.908)
  Pallas kernels: 38.7 us -> 35 us
    pallas_call x1, Pallas kernels: 38.7 us -> 35 us  [body(): pl.pallas_call(kernel, out_shape=pltpu.VMEM((32, 128), bf16), in_specs=[p...]
where the time goes in v3:
time: 36.5 us; the launch traced here: 36.3 us
  Pallas kernels  35 us (96%)
  between operations  0.66 us (2%)
  local copies, waits for them, and re-layouts  0.62 us (2%)
    pallas_call x1, Pallas kernels, body(): pl.pallas_call(kernel, out_shape=pltpu.VMEM((32, 128), bf16), in_specs=[p...  35 us

profile of v3, /device:TPU:1, one launch (start us, length us, event | category | flops | bytes accessed | tf_op | source)
XLA Modules:
  0.0 36.3 jit_solution(13393985918517747886)
XLA Ops:
  0.7 35.0 %shard_map.73 = bf16[32,128]{1,0:T(8,128)(2,1)S(1)} custom-call(s32[1]{0:T(128)S(6)} %copy.8.span_ref, bf16[1,1,4096]{2,1,0:T(2,128)(2,1)} %qn_hbm.1, bf16[1,1,2048]{2,1,0:T(2,128)(2,1)} %qr_hbm.1, bf16[1,128,512]{2,1,0:T(8,128)(2,1)} %lat_hbm.1, bf16[1,64,128]{2,1,0:T(8,128)(2,1)} %bitcast.1, bf16[32,128,512]{2,1,0:T(8,128)(2,1)} %kw_hbm.1, ...), custom_call_target="tpu_custom_call" | custom-call | flops 2415919104 | bytes 5242880 | tf_op jit(solution)/shard_map/pallas_call | solution.py:318
  35.7 0.6 %reshape.3 = bf16[1,1,4096]{2,1,0:T(2,128)(2,1)} reshape(bf16[32,128]{1,0:T(8,128)(2,1)S(1)} %shard_map.73) | data formatting | bytes 16384 | tf_op jit(solution)/shard_map/reshape | solution.py:337

commit v4 on v3

--- a/solution.py
+++ b/solution.py
@@ -267,20 +267,23 @@
     absorb(1)
     for block in range(SIDE // BLOCK):
         attend(1, block, 0, 3, True)
-    loads[5].wait()
-    far_partials = send_partials(1)
     last = []
     for part in range(PARTS):
         for d in range(2):
             hop2[d, part].wait_recv()
             last.append(pair(3 + d, part))
+    loads[5].wait()
+    far_partials = send_partials(1)
     for copy in last:
         copy.wait_recv()
     for slot in (3, 4):
         double_keys(slot)
     for block in range(SIDE // BLOCK):
         attend(0, block, 3, 5, False)
+    early = list(started)
     own_partials = send_partials(0)
+    for copy in early:
+        copy.wait_send()
 
     def merge_plane(side):
         for core in range(2):
@@ -302,13 +305,15 @@
     merge_plane(0)
     finals.append(start(remote(mm.at[0, 1 - c], fin.at[0, c], f_send.at[2], f_recv.at[2], other)))
     fin[0, c] = mm[0, c]
+    for copy in own_partials:
+        copy.wait_send()
     for copy in finals:
         copy.wait_recv()
     for half in range(2):
         num, _, den = merge([(fin[source, half, 0:16, :], fin[source, half, 16:32, :], 0) for source in range(2)])
         out_ref[half * 16 : half * 16 + 16, :] = (num / den).astype(bf16)
 
-    for copy in started:
+    for copy in finals:
         copy.wait_send()
 
 

time: 36.5 us -> 36.3 us (level)
  no operation moved by 1% of the time
where the time goes in v4:
time: 36.3 us; the launch traced here: 36.1 us
  Pallas kernels  34.8 us (96%)
  between operations  0.66 us (2%)
  local copies, waits for them, and re-layouts  0.62 us (2%)
    pallas_call x1, Pallas kernels, body(): pl.pallas_call(kernel, out_shape=pltpu.VMEM((32, 128), bf16), in_specs=[p...  34.8 us

profile of v4, /device:TPU:1, one launch (start us, length us, event | category | flops | bytes accessed | tf_op | source)
XLA Modules:
  0.0 36.1 jit_solution(17779452569750875126)
XLA Ops:
  0.7 34.8 %shard_map.73 = bf16[32,128]{1,0:T(8,128)(2,1)S(1)} custom-call(s32[1]{0:T(128)S(6)} %copy.8.span_ref, bf16[1,1,4096]{2,1,0:T(2,128)(2,1)} %qn_hbm.1, bf16[1,1,2048]{2,1,0:T(2,128)(2,1)} %qr_hbm.1, bf16[1,128,512]{2,1,0:T(8,128)(2,1)} %lat_hbm.1, bf16[1,64,128]{2,1,0:T(8,128)(2,1)} %bitcast.1, bf16[32,128,512]{2,1,0:T(8,128)(2,1)} %kw_hbm.1, ...), custom_call_target="tpu_custom_call" | custom-call | flops 2415919104 | bytes 5242880 | tf_op jit(solution)/shard_map/pallas_call | solution.py:323
  35.5 0.6 %reshape.3 = bf16[1,1,4096]{2,1,0:T(2,128)(2,1)} reshape(bf16[32,128]{1,0:T(8,128)(2,1)S(1)} %shard_map.73) | data formatting | bytes 16384 | tf_op jit(solution)/shard_map/reshape | solution.py:342

commit v5 on v4

--- a/solution.py
+++ b/solution.py
@@ -242,13 +242,13 @@
                 at = slice(rows.start + 16 * core, rows.start + 16 * core + 16)
                 stats += [m_s[at, :], l_s[at, :]]
             of[pl.ds(32 + h, 16, stride=48), :] = pack_stats(stats)
-        so[side] = of[...].reshape(16, 48, 128).astype(bf16)
         copies = []
         for i, (to, p) in enumerate(peers):
+            so[side, p] = of[pl.ds(pl.multiple_of(48 * p, 16), 48), :].astype(bf16)
             copies.append(
                 start(remote(so.at[side, p], ro.at[side, me], o_send.at[side, i], o_recv.at[side, i], to))
             )
-        ro[side, me] = so[side, me]
+        ro[side, me] = of[pl.ds(pl.multiple_of(48 * me, 16), 48), :].astype(bf16)
         return copies
 
     loads[4].wait()

time: 36.3 us -> 36.3 us (level)
  no operation moved by 1% of the time
where the time goes in v5:
time: 36.3 us; the launch traced here: 36.1 us
  Pallas kernels  34.8 us (96%)
  between operations  0.66 us (2%)
  local copies, waits for them, and re-layouts  0.62 us (2%)
    pallas_call x1, Pallas kernels, body(): pl.pallas_call(kernel, out_shape=pltpu.VMEM((32, 128), bf16), in_specs=[p...  34.8 us

profile of v5, /device:TPU:1, one launch (start us, length us, event | category | flops | bytes accessed | tf_op | source)
XLA Modules:
  0.0 36.1 jit_solution(15639504252620689361)
XLA Ops:
  0.7 34.8 %shard_map.73 = bf16[32,128]{1,0:T(8,128)(2,1)S(1)} custom-call(s32[1]{0:T(128)S(6)} %copy.8.span_ref, bf16[1,1,4096]{2,1,0:T(2,128)(2,1)} %qn_hbm.1, bf16[1,1,2048]{2,1,0:T(2,128)(2,1)} %qr_hbm.1, bf16[1,128,512]{2,1,0:T(8,128)(2,1)} %lat_hbm.1, bf16[1,64,128]{2,1,0:T(8,128)(2,1)} %bitcast.1, bf16[32,128,512]{2,1,0:T(8,128)(2,1)} %kw_hbm.1, ...), custom_call_target="tpu_custom_call" | custom-call | flops 2415919104 | bytes 5242880 | tf_op jit(solution)/shard_map/pallas_call | solution.py:323
  35.5 0.6 %reshape.3 = bf16[1,1,4096]{2,1,0:T(2,128)(2,1)} reshape(bf16[32,128]{1,0:T(8,128)(2,1)S(1)} %shard_map.73) | data formatting | bytes 16384 | tf_op jit(solution)/shard_map/reshape | solution.py:342
